TPU v7x, 256 devices: a whole 4x4x8 slice. The times are simulated.
256 devices in a mesh: sub: 8 (over x, z_hi), ifc: 32 (over z_lo, y, core).
Axes of the slice: x: 4, y: 4, z: 8 (z_hi: 2, z_lo: 4; z = z_hi * 4 + z_lo), core: 2. Of those that a mesh axis runs over, the one named last changes fastest.
Arguments:
- stretch_store: bfloat16 [8, 32, 512, 1024], P('sub', 'ifc'), may hold values from -6 to 6
- stretch_owner: int32 [8, 2], P('sub'), may hold values from 0 to 31, as said below
- tile_map: int32 [8, 64, 2, 8], P('sub', 'ifc'), may hold values from 0 to 4
- inverse_block: bfloat16 [8, 64, 1024, 1024], P('sub', 'ifc'), may hold values from -0.1875 to 0.1875
- face_coupling: bfloat16 [8, 64, 1024, 128], P('sub', 'ifc'), may hold values from -0.1875 to 0.1875
- row_offset: int32 [8, 64], P('sub', 'ifc'), may hold values from 0 to 4064, as said below
- row_count: int32 [8, 64], P('sub', 'ifc'), may hold values from 32 to 128, as said below
- interface_block: float32 [4096, 2048], P('ifc', 'sub'), may hold values from -6 to 6
Outputs:
- schur: float32 [4096, 2048], P('ifc', 'sub')
Inputs may be any that keep to these rules, and one draw needn't show every extreme that they name: `stretch_owner`: the two owners of one sub index differ. With p = j // 2, the subdomain at index j of the second dimension starts between max(0, p * 128 - 128 // 2) and p * 128 + 128 // 2, and row_offset + row_count <= min(4096, (p + 2) * 128). `row_count`: some subdomain has exactly 128 rows.
All inputs are finite; a program needn't handle non-finite values.
Results may differ from a plain program's by a relative error of at most 0.0027.
Values may be sent and summed in bfloat16 or wider, within the bound.
A program may use at most 64 MiB of HBM per device.

v0:
```python
import jax
import jax.numpy as jnp
from jax import lax
from jax.sharding import PartitionSpec as P

TR = 128
NT = 4


def passed_along(value, axis, steps):
    count = lax.axis_size(axis)
    initial, last = (max(0, -steps), min(count, count - steps))
    return lax.ppermute(value, axis, [(source, source + steps) for source in range(initial, last)])


def spread(value, axis, source):
    kept = jnp.where(lax.axis_index(axis) == source, value, 0).astype(value.dtype)
    return lax.psum(kept, axis)


def neighbours(band_rows):
    owner_rows = band_rows.shape[0] // 3
    middle = band_rows[owner_rows : 2 * owner_rows]
    lower_part = passed_along(band_rows[2 * owner_rows :], "ifc", 1)
    upper_part = passed_along(band_rows[:owner_rows], "ifc", -1)
    return middle + lower_part + upper_part


def per_device(
    stretch_store,
    stretch_owner,
    tile_map,
    inverse_block,
    face_coupling,
    row_offset,
    row_count,
    interface_block,
):
    own_store = stretch_store[0, 0]
    width_stretch = own_store.shape[1]
    interior = inverse_block.shape[2]
    owner_rows = face_coupling.shape[3]
    local_count = inverse_block.shape[1]
    stores = []
    for k in range(2):
        received = spread(own_store, "ifc", stretch_owner[0, k])
        stores.append(received.reshape(NT, TR, width_stretch))
    position = lax.axis_index("ifc")
    band_rows = jnp.zeros((3 * owner_rows, 2 * width_stretch), jnp.float32)
    for local in range(local_count):
        pieces = []
        for k in range(2):
            onehot = (
                tile_map[0, local, k][:, None] == jnp.arange(NT, dtype=jnp.int32)[None, :]
            ).astype(jnp.bfloat16)
            picked = jnp.einsum(
                "it,trw->irw", onehot, stores[k], preferred_element_type=jnp.float32
            )
            pieces.append(picked.astype(jnp.bfloat16).reshape(interior, width_stretch))
        coupling = jnp.concatenate(pieces, axis=1)
        solved = jnp.dot(
            inverse_block[0, local], coupling, preferred_element_type=jnp.float32
        ).astype(jnp.bfloat16)
        partial_value = lax.dot_general(
            face_coupling[0, local],
            solved,
            (((0,), (0,)), ((), ())),
            preferred_element_type=jnp.float32,
        )
        live_rows = jnp.arange(owner_rows, dtype=jnp.int32)[:, None] < row_count[0, local]
        partial_value = jnp.where(live_rows, partial_value, jnp.float32(0.0))
        band_start = row_offset[0, local] - (position - 1) * owner_rows
        zero_col = jnp.zeros((), jnp.int32)
        current = lax.dynamic_slice(
            band_rows, (band_start, zero_col), (owner_rows, 2 * width_stretch)
        )
        band_rows = lax.dynamic_update_slice(
            band_rows, current + partial_value, (band_start, zero_col)
        )
    gathered_rows = neighbours(band_rows)
    summed = lax.psum_scatter(gathered_rows, "sub", scatter_dimension=1, tiled=True)
    return interface_block - summed


def solution(mesh):
    return jax.shard_map(
        per_device,
        mesh=mesh,
        in_specs=(
            P("sub", "ifc", None, None),
            P("sub", None),
            P("sub", "ifc", None, None),
            P("sub", "ifc", None, None),
            P("sub", "ifc", None, None),
            P("sub", "ifc"),
            P("sub", "ifc"),
            P("ifc", "sub"),
        ),
        out_specs=P("ifc", "sub"),
        check_vma=False,
    )
```

profile of v0, /device:TPU:1, one launch (start us, length us, event | category | flops | bytes accessed | tf_op | source)
XLA Modules:
  0.0 465.7 jit_solution(13133127079757810659)
XLA Ops:
  6.5 0.0 all-reduce.3.cloned.1.call-start
  6.5 1.3 fusion.71
  9.0 1.4 broadcast_select_fusion.1
  10.4 0.0 copy-start.4
  10.4 0.0 copy-start.5
  10.4 0.0 copy-start.3
  10.4 1.8 copy.11
  12.2 1.8 copy.13
  14.1 0.0 all-reduce.3.cloned.1.call-update
  14.1 0.0 reduce-scatter.2.cloned.1.call-start
  14.1 0.0 copy-done.4
  14.1 0.6 fusion.70
  16.0 0.0 copy-done.5
  16.0 0.6 fusion.69
  16.6 0.6 iota_compare_fusion.5
  17.3 0.7 iota_compare_fusion.4
  17.9 0.0 copy-done.3
  17.9 282.2 %all-reduce.3.cloned.1.call-done = (bf16[4,128,1024]{2,0,1:T(4,128)(2,1)}, bf16[4,128,1024]{2,0,1:T(4,128)(2,1)}) async-done(((bf16[4,128,1024]{2,0,1:T(4,128)(2,1)}, bf16[4,128,1024]{2,0,1:T(4,128)(2,1)}), (bf16[4,128,1024]{2,0,1:T(4,128)(2,1)}, bf16[4,128,1024]{2,0,1:T(4,128)(2,1)})) %all-reduce.3.cloned.1.call-update) | async-done | bytes 2097168 | tf_op jit(solution)/shard_map/psum | solution.py:18
  300.1 2.2 convolution_convert_fusion.2
  302.3 1.2 copy.14
  303.5 0.0 copy-done.1
  303.5 1.3 convolution_convert_fusion.3
  304.7 2.5 copy.12
  307.2 0.0 copy-start
  307.3 1.1 convolution_convert_fusion.1
  308.3 2.5 copy.15
  310.8 0.0 copy-done
  310.8 1.1 convolution_convert_fusion
  311.9 2.5 copy.16
  314.4 0.0 copy-done.6
  314.4 9.0 %fusion.15 = f32[128,2048]{0,1:T(8,128)} fusion(bf16[1024,1024]{1,0:T(8,128)(2,1)S(1)} %bitcast.64, bf16[1024,1024]{1,0:T(8,128)(2,1)} %bitcast.66, bf16[1,2,1024,1024]{3,2,1,0:T(8,128)(2,1)} %param.11, pred[128]{0:T(512)(128)(4,1)S(1)} %iota_compare_fusion.5, bf16[1,2,1024,128]{3,2,1,0:T(8,128)(2,1)S(1)} %copy-done.6), kind=kOutput, calls=%fused_computation.13 | convolution fusion | flops 4842586112 | bytes 7602688 | tf_op jit(solution)/shard_map/dot_general | solution.py:64
  323.4 0.2 broadcast_in_dim.32
  323.6 10.5 %dynamic_update_slice.6 = f32[384,2048]{0,1:T(8,128)S(1)} dynamic-update-slice(f32[384,2048]{0,1:T(8,128)S(1)} %broadcast_in_dim.32, f32[128,2048]{0,1:T(8,128)} %fusion.15, s32[]{:T(128)S(6)} %select_n.48, s32[]{:T(128)} %constant.16.clone.1) | dynamic-update-slice | bytes 2097156 | tf_op jit(solution)/shard_map/dynamic_update_slice | solution.py:77
  334.1 9.7 %fusion.24 = f32[128,2048]{0,1:T(8,128)} fusion(bf16[1024,1024]{1,0:T(8,128)(2,1)} %bitcast.67, bf16[1024,1024]{1,0:T(8,128)(2,1)} %bitcast.65, bf16[1,2,1024,1024]{3,2,1,0:T(8,128)(2,1)} %param.11, f32[384,2048]{0,1:T(8,128)S(1)} %dynamic_update_slice.6, s32[]{:T(128)S(6)} %select_n.49, pred[128]{0:T(512)(128)(4,1)S(1)} %iota_compare_fusion.4, ...), kind=kOutput, calls=%fused_computation.16 | convolution fusion | flops 4842848256 | bytes 8650884 | tf_op jit(solution)/shard_map/dot_general | solution.py:64
  343.7 10.2 %dynamic_update_slice.7 = f32[384,2048]{0,1:T(8,128)S(1)} dynamic-update-slice(f32[384,2048]{0,1:T(8,128)S(1)} %dynamic_update_slice.6, f32[128,2048]{0,1:T(8,128)} %fusion.24, s32[]{:T(128)S(6)} %select_n.49, s32[]{:T(128)} %constant.16.clone.1) | dynamic-update-slice | bytes 2097156 | tf_op jit(solution)/shard_map/dynamic_update_slice | solution.py:77
  353.9 0.1 fusion.68
  354.1 0.0 copy-start.2
  354.1 2.1 collective-permute-start
  356.1 2.5 collective-permute-start.1
  358.6 9.2 %collective-permute-done = f32[128,2048]{0,1:T(8,128)S(1)} collective-permute-done((f32[128,2048]{0,1:T(8,128)S(1)}, f32[128,2048]{0,1:T(8,128)S(1)}, u32[]{:S(2)}, u32[]{:S(2)}) %collective-permute-start) | collective-permute-done | bytes 1048608 | tf_op jit(solution)/shard_map/ppermute | solution.py:13
  367.9 4.4 collective-permute-done.1
  372.3 1.2 fusion.47
  373.5 0.0 reduce-scatter.2.cloned.1.call-update
  373.5 0.0 copy-done.2
  373.5 0.1 copy.17
  373.6 83.6 %reduce-scatter.2.cloned.1.call-done = f32[128,256]{0,1:T(8,128)} async-done(((f32[128,2048]{0,1:T(8,128)}), f32[128,256]{0,1:T(8,128)}) %reduce-scatter.2.cloned.1.call-update) | async-done | bytes 131088 | tf_op jit(solution)/shard_map/reduce_scatter | solution.py:81
  457.2 0.9 sub.16
  458.1 0.8 copy.18
  (3 shorter events, 0.0 us)
Async XLA Ops:
  6.5 293.6 %all-reduce.3.cloned.1.call-start = ((), (), s32[]{:S(2)}) async-start(), calls=%async_computation.2 | async-start | bytes 4194304 | tf_op jit(solution)/shard_map/psum | solution.py:18
  10.4 3.8 copy-start.4
  10.4 5.6 %copy-start.5 = (s32[1,2]{1,0:T(1,128)S(1)}, s32[1,2]{1,0:T(1,128)}, u32[]{:S(2)}) copy-start(s32[1,2]{1,0:T(1,128)} %param.14) | copy-start | bytes 28
  10.4 7.5 %copy-start.3 = (s32[1,2,2,8]{3,2,1,0:T(2,128)S(1)}, s32[1,2,2,8]{3,2,1,0:T(2,128)}, u32[]{:S(2)}) copy-start(s32[1,2,2,8]{3,2,1,0:T(2,128)} %param.10) | copy-start | bytes 388
  14.1 443.1 %reduce-scatter.2.cloned.1.call-start = ((), (), s32[]{:S(2)}) async-start(), calls=%async_computation.1 | async-start | bytes 1179648 | tf_op jit(solution)/shard_map/reduce_scatter | solution.py:81
  300.1 3.3 copy-start.1
  307.2 3.6 copy-start
  310.8 3.5 copy-start.6
  354.1 19.4 %copy-start.2 = (f32[128,256]{1,0:T(8,128)S(1)}, f32[128,256]{1,0:T(8,128)}, u32[]{:S(2)}) copy-start(f32[128,256]{1,0:T(8,128)} %param.15) | copy-start | bytes 393220
  354.1 13.8 %collective-permute-start = (f32[128,2048]{0,1:T(8,128)S(1)}, f32[128,2048]{0,1:T(8,128)S(1)}, u32[]{:S(2)}, u32[]{:S(2)}) collective-permute-start(f32[128,2048]{0,1:T(8,128)S(1)} %get-tuple-element.7), channel_id=1, source_target_pairs={{0,1},{1,2},{2,3},{3,4},{4,5},{5,6},{6,7},{7,8},{8,9},{9,10},{10,1... | collective-permute-start | bytes 3145736 | tf_op jit(solution)/shard_map/ppermute | solution.py:13
  356.1 16.1 %collective-permute-start.1 = (f32[128,2048]{0,1:T(8,128)S(1)}, f32[128,2048]{0,1:T(8,128)S(1)}, u32[]{:S(2)}, u32[]{:S(2)}) collective-permute-start(f32[128,2048]{0,1:T(8,128)S(1)} %get-tuple-element.8), channel_id=1, source_target_pairs={{1,0},{2,1},{3,2},{4,3},{5,4},{6,5},{7,6},{8,7},{9,8},{10,9},{11,1... | collective-permute-start | bytes 3145736 | tf_op jit(solution)/shard_map/ppermute | solution.py:13
Sparse Core Ops, SparseCore 0:
  14.2 285.8 all-reduce.2
  373.6 83.5 reduce-scatter.1
where the time goes:
time: 467 us; the launch traced here: 466 us
  waiting for transfers between devices  379 us (81%)
  local copies, waits for them, and re-layouts  36.6 us (8%)
  matrix products  24.2 us (5%)
  between operations  16.1 us (3%)
  other arithmetic  4.76 us (1%)
    psum x1, waiting for transfers between devices, spread(): return lax.psum(kept, axis)  282 us
    reduce_scatter x1, waiting for transfers between devices, per_device(): lax.psum_scatter(gathered_rows, 'sub', scatter_dimension=1, tiled=True)  83.6 us
    dynamic_update_slice x2, local copies, waits for them, and re-layouts, per_device(): lax.dynamic_update_slice(band_rows, current + partial_value, (band_start,...  20.6 us
    dot_general x2, matrix products, per_device(): lax.dot_general(face_coupling[0, local], solved, (((0,), (0,)), ((), ()))...  18.7 us
    ppermute x2, waiting for transfers between devices, passed_along(): lax.ppermute(value, axis, [(source, source + steps) for source in range(i...  13.6 us
  transfers between devices with their start and end apart: 4, of which 4 were waited for; matrix products, arithmetic and copies ran while one was open for 1% of the time, Pallas kernels for 0%

commit v1 on v0

v1 whole, which is shorter than its diff:
```python
import jax
import jax.numpy as jnp
from jax import lax
from jax.experimental import pallas as pl
from jax.experimental.pallas import tpu as pltpu
from jax.sharding import PartitionSpec as P

MESH = pl.DeviceIdType.MESH
F32 = jnp.float32
BF16 = jnp.bfloat16
NT_DIMS = (((1,), (1,)), ((), ()))


def aligned(value, unit):
    return pl.multiple_of(value, unit)


def kernel(
    owner_ref,
    map_ref,
    offset_ref,
    count_ref,
    store_ref,
    inverse_ref,
    face_ref,
    iface_ref,
    out_ref,
    st,
    inv,
    face,
    iface,
    r1_first,
    r1_second,
    s2,
    r2,
    m2,
    r3,
    m3,
    r4,
    bmat,
    placed,
    gband,
    band,
    nb,
    hs,
    hf,
    pmat,
    late,
    cross,
    load_sem,
    s1_send,
    s1_recv,
    s2_send,
    s2_recv,
    s3_send,
    s3_recv,
    s4_send,
    s4_recv,
    s5_send,
    s5_recv,
    s6_send,
    s6_recv,
    nb_send,
    nb_recv,
    h_send,
    h_recv,
    late_send,
    late_recv,
):
    sub = lax.axis_index("sub")
    ifc = lax.axis_index("ifc")
    x, zh = sub // 2, sub % 2
    zl, y, c = ifc // 8, (ifc // 2) % 4, ifc % 2

    def flip(value, mask):
        out = 0
        for bit in (1, 2):
            digit = (value // bit) % 2
            out = out + bit * ((1 - digit) if mask & bit else digit)
        return out

    def device(x_, zh_, zl_, y_, c_):
        return (x_ * 2 + zh_, zl_ * 8 + y_ * 2 + c_)

    oc = 1 - c
    r1 = (r1_first, r1_second)
    first_partner = (flip(y, 1), flip(y, 3))
    second_partner = (flip(y, 3), flip(y, 1))
    y0, y1 = y % 2, y // 2
    half = ((y0 + y1) % 2, y1)
    quarter = (y1, y0)

    partners = [device(x, zh, zl, y, oc)]
    for h in range(2):
        for core in (c, oc):
            partners.append(device(x, zh, zl, first_partner[h], core))
    for a in range(4):
        for b in range(4):
            if a or b:
                partners.append(device(flip(x, a), zh, flip(zl, b), y, c))
    for a in range(1, 4):
        partners.append(device(flip(x, a), zh, zl, y, oc))
    before, after = lax.rem(ifc + 31, 32), lax.rem(ifc + 1, 32)
    partners.append((sub, before))
    partners.append((sub, after))
    for core in (c, oc):
        partners.append(device(x, 1 - zh, zl, y, core))
    barrier = pltpu.get_barrier_semaphore()
    for partner in partners:
        pl.semaphore_signal(barrier, inc=1, device_id=partner, device_id_type=MESH)

    loads = []
    face_load = pltpu.make_async_copy(face_ref.at[0], face, load_sem.at[0])
    face_load.start()
    inv_loads = []
    for l in range(2):
        cp = pltpu.make_async_copy(inverse_ref.at[0, l], inv.at[l], load_sem.at[1 + l])
        cp.start()
        inv_loads.append(cp)
    n = 3
    for j in range(2):
        for xh in range(2):
            for cc in range(2):
                cp = pltpu.make_async_copy(
                    store_ref.at[0, 0, :, pl.ds(xh * 512 + j * 256 + cc * 128, 128)],
                    st.at[j, xh, cc],
                    load_sem.at[n],
                )
                cp.start()
                loads.append(cp)
                n += 1
    iface_load = pltpu.make_async_copy(iface_ref, iface, load_sem.at[n])
    iface_load.start()

    face_load.wait()
    row_at = lax.broadcasted_iota(jnp.int32, (256, 128), 0)
    col_at = lax.broadcasted_iota(jnp.int32, (256, 128), 1)
    for l in range(2):
        start = offset_ref[0, l] - (ifc * 128 - 64)
        here = jnp.logical_and(row_at == col_at + start, col_at < count_ref[0, l])
        place = jnp.where(here, 1.0, 0.0).astype(BF16)
        placed[l] = lax.dot_general(
            place, face[l], NT_DIMS, preferred_element_type=F32
        ).astype(BF16)
    for l in range(2):
        inv_loads[l].wait()

        def columns(i, _):
            at = pl.ds(aligned(i * 256, 256), 256)
            gband[l, :, at] = jnp.dot(
                placed[l], inv[l, :, at], preferred_element_type=F32
            )
            return 0

        lax.fori_loop(0, 4, columns, 0)

    def fold(r, _):
        rows = pl.ds(aligned(r * 64, 64), 64)
        for k in range(2):
            for t in range(4):
                acc = jnp.zeros((64, 128), F32)
                for l in range(2):
                    for i in range(8):
                        weight = jnp.where(map_ref[0, l, k, i] == t, 1.0, 0.0)
                        acc = acc + weight * gband[l, rows, i * 128 : (i + 1) * 128]
                at = k * 512 + t * 128
                band[rows, at : at + 128] = acc
        return 0

    lax.fori_loop(0, 4, fold, 0)

    for cp in loads:
        cp.wait()
    steps = ((1 - zh), zh)
    for n in range(2):
        for h in range(2):
            rows = pl.ds(aligned(h * 256 + half[h] * 128, 128), 128)
            r1[n][h, 0] = st[steps[n], :, c, rows, :]
            r1[n][h, 4] = jnp.zeros((2, 128, 128), BF16)

    picks = []
    for h in range(2):
        row = []
        for k in range(2):
            o = owner_ref[0, k]
            pick = jnp.int32(4)
            sources = (
                zl * 8 + y * 2 + c,
                zl * 8 + y * 2 + oc,
                zl * 8 + first_partner[h] * 2 + c,
                zl * 8 + first_partner[h] * 2 + oc,
            )
            for at, source in enumerate(sources):
                pick = jnp.where(o == source, at, pick)
            row.append(pick)
        picks.append(row)

    started = []

    def send(src, dst, send_sem, recv_sem, to):
        cp = pltpu.make_async_remote_copy(
            src_ref=src,
            dst_ref=dst,
            send_sem=send_sem,
            recv_sem=recv_sem,
            device_id=to,
            device_id_type=MESH,
        )
        cp.start()
        started.append(cp)
        return cp

    pl.semaphore_wait(barrier, len(partners))

    def stage1(n):
        cps = []
        for h in range(2):
            rows = pl.ds(aligned(h * 256 + (1 - half[h]) * 128, 128), 128)
            for d, core in enumerate((c, oc)):
                cps.append(
                    send(
                        st.at[steps[n], :, core, rows, :],
                        r1[n].at[h, 2 + d],
                        s1_send.at[n, h, d],
                        s1_recv.at[n, h, d],
                        device(x, zh, zl, first_partner[h], core),
                    )
                )
            rows = pl.ds(aligned(h * 256 + half[h] * 128, 128), 128)
            cps.append(
                send(
                    st.at[steps[n], :, oc, rows, :],
                    r1[n].at[h, 1],
                    s1_send.at[n, h, 2],
                    s1_recv.at[n, h, 2],
                    device(x, zh, zl, y, oc),
                )
            )
        return cps

    def stage2(n, cps):
        out = []
        for cp in cps:
            cp.wait_recv()
        for h in range(2):
            rows = pl.ds(aligned((1 - quarter[h]) * 64, 64), 64)
            for k in range(2):
                s2[n, h, 2 * k : 2 * k + 2] = r1[n][h, picks[h][k], :, rows, :]
            out.append(
                send(
                    s2.at[n, h],
                    r2.at[n, h],
                    s2_send.at[n, h],
                    s2_recv.at[n, h],
                    device(x, zh, zl, second_partner[h], c),
                )
            )
        return out

    def stage3(n, cps):
        out = []
        for cp in cps:
            cp.wait_recv()
        for h in range(2):
            rows = pl.ds(aligned(quarter[h] * 64, 64), 64)
            for k in range(2):
                m2[n, h, 2 * k : 2 * k + 2] = (
                    r1[n][h, picks[h][k], :, rows, :] + r2[n, h, 2 * k : 2 * k + 2]
                )
        for d in range(1, 4):
            to = flip(zl, d)
            out.append(
                send(
                    m2.at[n, :, :, pl.ds(aligned(to * 16, 16), 16), :],
                    r3.at[n, d],
                    s3_send.at[n, d],
                    s3_recv.at[n, d],
                    device(x, zh, to, y, c),
                )
            )
        return out

    def stage4(n, cps):
        out = []
        for cp in cps:
            cp.wait_recv()
        rows = pl.ds(aligned(zl * 16, 16), 16)
        m3[n] = m2[n, :, :, rows, :] + r3[n, 1] + r3[n, 2] + r3[n, 3]
        for a in range(4):
            for b in range(4):
                if a or b:
                    out.append(
                        send(
                            m3.at[n, :, flip(x, a)],
                            r4.at[n, x, :, rows, :],
                            s4_send.at[n, a, b],
                            s4_recv.at[n, a, b],
                            device(flip(x, a), zh, flip(zl, b), y, c),
                        )
                    )
        r4[n, x, :, rows, :] = m3[n, :, x]
        return out

    def stage5(n, cps):
        out = []
        for cp in cps:
            cp.wait_recv()
        for h in range(2):
            rows = pl.ds(aligned(h * 256 + half[h] * 128 + quarter[h] * 64, 64), 64)
            out.append(
                send(
                    r4.at[n, :, h],
                    bmat.at[n, :, rows, :],
                    s5_send.at[n, h],
                    s5_recv.at[n, h],
                    device(x, zh, zl, second_partner[h], c),
                )
            )
            bmat[n, :, rows, :] = r4[n, :, h]
        return out

    def stage6(n, cps):
        out = []
        for cp in cps:
            cp.wait_recv()
        for h in range(2):
            rows = pl.ds(aligned(h * 256 + half[h] * 128, 128), 128)
            out.append(
                send(
                    bmat.at[n, :, rows, :],
                    bmat.at[n, :, rows, :],
                    s6_send.at[n, h],
                    s6_recv.at[n, h],
                    device(x, zh, zl, first_partner[h], c),
                )
            )
        return out

    def product(n, cps):
        for cp in cps:
            cp.wait_recv()
        total = jnp.zeros((256, 128), F32)
        for at in range(4):
            total = total + jnp.dot(hf[at], bmat[n, at], preferred_element_type=F32)
        pmat[n] = total

    a1 = stage1(0)
    nb_cps = [
        send(band.at[0:64], nb.at[1], nb_send.at[0], nb_recv.at[0], (sub, before)),
        send(band.at[192:256], nb.at[0], nb_send.at[1], nb_recv.at[1], (sub, after)),
    ]
    b1 = stage1(1)
    a2 = stage2(0, a1)

    for cp in nb_cps:
        cp.wait_recv()
    for k in range(2):
        at = slice(k * 512, (k + 1) * 512)
        hs[k, 0:64] = (band[64:128, at] + nb[0, :, at]).astype(BF16)
        hs[k, 64:128] = (band[128:192, at] + nb[1, :, at]).astype(BF16)
    own_rows = pl.ds(aligned(c * 128, 128), 128)
    h_cps = []
    for a in range(4):
        for d, core in enumerate((c, oc)):
            if a or d:
                h_cps.append(
                    send(
                        hs.at[flip(x, a) // 2],
                        hf.at[x, own_rows, :],
                        h_send.at[a, d],
                        h_recv.at[a, d],
                        device(flip(x, a), zh, zl, y, core),
                    )
                )
    hf[x, own_rows, :] = hs[x // 2]

    b2 = stage2(1, b1)
    a3 = stage3(0, a2)
    b3 = stage3(1, b2)
    a4 = stage4(0, a3)
    b4 = stage4(1, b3)
    a5 = stage5(0, a4)
    b5 = stage5(1, b4)
    a6 = stage6(0, a5)
    b6 = stage6(1, b5)
    for cp in h_cps:
        cp.wait_recv()
    product(0, a6)
    late_cps = []
    for d, core in enumerate((c, oc)):
        late_cps.append(
            send(
                pmat.at[0, pl.ds(aligned(core * 128, 128), 128), :],
                late.at[d],
                late_send.at[d],
                late_recv.at[d],
                device(x, 1 - zh, zl, y, core),
            )
        )
    product(1, b6)
    late_cps.append(
        send(
            pmat.at[1, pl.ds(aligned(oc * 128, 128), 128), :],
            cross,
            late_send.at[2],
            late_recv.at[2],
            device(x, zh, zl, y, oc),
        )
    )
    iface_load.wait()
    for cp in late_cps:
        cp.wait_recv()
    own = pl.ds(aligned(c * 128, 128), 128)
    other = pl.ds(aligned(oc * 128, 128), 128)
    out_ref[:, own] = iface[:, own] - (pmat[1, own, :] + late[0])
    out_ref[:, other] = iface[:, other] - (cross[...] + late[1])
    for cp in started:
        cp.wait_send()


def per_device(
    stretch_store,
    stretch_owner,
    tile_map,
    inverse_block,
    face_coupling,
    row_offset,
    row_count,
    interface_block,
):
    smem = pl.BlockSpec(memory_space=pltpu.SMEM)
    anywhere = pl.BlockSpec(memory_space=pl.ANY)
    dma = pltpu.SemaphoreType.DMA
    return pl.pallas_call(
        kernel,
        out_shape=jax.ShapeDtypeStruct((128, 256), F32),
        in_specs=[smem] * 4 + [anywhere] * 4,
        out_specs=pl.BlockSpec(memory_space=pltpu.VMEM),
        scratch_shapes=[
            pltpu.VMEM((2, 2, 2, 512, 128), BF16),
            pltpu.VMEM((2, 1024, 1024), BF16),
            pltpu.VMEM((2, 1024, 128), BF16),
            pltpu.VMEM((128, 256), F32),
            pltpu.VMEM((2, 5, 2, 128, 128), BF16),
            pltpu.VMEM((2, 5, 2, 128, 128), BF16),
            pltpu.VMEM((2, 2, 4, 64, 128), BF16),
            pltpu.VMEM((2, 2, 4, 64, 128), BF16),
            pltpu.VMEM((2, 2, 4, 64, 128), BF16),
            pltpu.VMEM((2, 4, 2, 4, 16, 128), BF16),
            pltpu.VMEM((2, 2, 4, 16, 128), BF16),
            pltpu.VMEM((2, 4, 2, 64, 128), BF16),
            pltpu.VMEM((2, 4, 512, 128), BF16),
            pltpu.VMEM((2, 256, 1024), BF16),
            pltpu.VMEM((2, 256, 1024), F32),
            pltpu.VMEM((256, 1024), F32),
            pltpu.VMEM((2, 64, 1024), F32),
            pltpu.VMEM((2, 128, 512), BF16),
            pltpu.VMEM((4, 256, 512), BF16),
            pltpu.VMEM((2, 256, 128), F32),
            pltpu.VMEM((2, 128, 128), F32),
            pltpu.VMEM((128, 128), F32),
            dma((12,)),
            dma((2, 2, 3)),
            dma((2, 2, 3)),
            dma((2, 2)),
            dma((2, 2)),
            dma((2, 4)),
            dma((2, 4)),
            dma((2, 4, 4)),
            dma((2, 4, 4)),
            dma((2, 2)),
            dma((2, 2)),
            dma((2, 2)),
            dma((2, 2)),
            dma((2,)),
            dma((2,)),
            dma((4, 2)),
            dma((4, 2)),
            dma((3,)),
            dma((3,)),
        ],
        compiler_params=pltpu.CompilerParams(
            collective_id=0, has_side_effects=True, vmem_limit_bytes=40 * 1024 * 1024
        ),
        name="schur",
    )(
        stretch_owner,
        tile_map,
        row_offset,
        row_count,
        stretch_store,
        inverse_block,
        face_coupling,
        interface_block,
    )


def solution(mesh):
    return jax.shard_map(
        per_device,
        mesh=mesh,
        in_specs=(
            P("sub", "ifc", None, None),
            P("sub", None),
            P("sub", "ifc", None, None),
            P("sub", "ifc", None, None),
            P("sub", "ifc", None, None),
            P("sub", "ifc"),
            P("sub", "ifc"),
            P("ifc", "sub"),
        ),
        out_specs=P("ifc", "sub"),
        check_vma=False,
    )
```

time: 467 us -> 65.9 us (0.14)
  waiting for transfers between devices: 379 us -> 0 us
  Pallas kernels: 0 us -> 57 us
  local copies, waits for them, and re-layouts: 36.6 us -> 8.66 us
  matrix products: 24.2 us -> 0 us
  between operations: 16.1 us -> 0.02 us
  other arithmetic: 4.76 us -> 0 us
    psum x1 -> x0, waiting for transfers between devices: 282 us -> none  [spread(): return lax.psum(kept, axis)]
    reduce_scatter x1 -> x0, waiting for transfers between devices: 83.6 us -> none  [per_device(): lax.psum_scatter(gathered_rows, 'sub', scatter_dimension=1, tiled=True)]
    pallas_call x0 -> x1, Pallas kernels: none -> 57 us  [per_device(): pl.pallas_call(kernel, out_shape=jax.ShapeDtypeStruct((128, 256), F32), i...]
    dot_general x6 -> x0, matrix products: 24.2 us -> none  [the longest x2 18.7 us: per_device(): lax.dot_general(face_coupling[0, local], solved, (((0,), (0,)), ((), ()))...]
    dynamic_update_slice x2 -> x0, local copies, waits for them, and re-layouts: 20.6 us -> none  [per_device(): lax.dynamic_update_slice(band_rows, current + partial_value, (band_start,...]
    ppermute x2 -> x0, waiting for transfers between devices: 13.6 us -> none  [passed_along(): lax.ppermute(value, axis, [(source, source + steps) for source in range(i...]
    convert_element_type x4 -> x0, local copies, waits for them, and re-layouts: 8.63 us -> none  [per_device(): pieces.append(picked.astype(jnp.bfloat16).reshape(interior, width_stretch))]
    unnamed x15 -> x17, local copies, waits for them, and re-layouts: 0.12 us -> 8.66 us
  transfers between devices with their start and end apart: 4 -> 0, of which waited for: 4 -> 0; matrix products, arithmetic and copies ran while one was open for 1% -> 0% of each run, Pallas kernels for 0% -> 0%
where the time goes in v1:
time: 65.9 us; the launch traced here: 65.7 us
  Pallas kernels  57 us (86%)
  local copies, waits for them, and re-layouts  8.66 us (13%)
    pallas_call x1, Pallas kernels, per_device(): pl.pallas_call(kernel, out_shape=jax.ShapeDtypeStruct((128, 256), F32), i...  57 us
    unnamed x17, local copies, waits for them, and re-layouts  8.66 us

profile of v1, /device:TPU:1, one launch (start us, length us, event | category | flops | bytes accessed | tf_op | source)
XLA Modules:
  0.0 65.7 jit_solution(17831508135815324748)
XLA Ops:
  0.0 0.0 copy-start
  0.0 2.2 %copy-done = bf16[1,2,1024,1024]{3,2,1,0:T(8,128)(2,1)S(1)} copy-done((bf16[1,2,1024,1024]{3,2,1,0:T(8,128)(2,1)S(1)}, bf16[1,2,1024,1024]{3,2,1,0:T(8,128)(2,1)}, u32[]{:S(2)}) %copy-start) | copy-done | bytes 4194328
  2.2 0.0 copy-start.1
  2.2 1.2 %copy-done.1 = bf16[1,1,512,1024]{3,2,1,0:T(8,128)(2,1)S(1)} copy-done((bf16[1,1,512,1024]{3,2,1,0:T(8,128)(2,1)S(1)}, bf16[1,1,512,1024]{3,2,1,0:T(8,128)(2,1)}, u32[]{:S(2)}) %copy-start.1) | copy-done | bytes 1048600
  3.4 0.0 copy-start.2
  3.4 1.0 %copy-done.2 = bf16[1,2,1024,128]{3,2,1,0:T(8,128)(2,1)S(1)} copy-done((bf16[1,2,1024,128]{3,2,1,0:T(8,128)(2,1)S(1)}, bf16[1,2,1024,128]{3,2,1,0:T(8,128)(2,1)}, u32[]{:S(2)}) %copy-start.2) | copy-done | bytes 524312
  4.5 0.0 copy-start.3
  4.5 0.9 %copy-done.3 = f32[128,256]{1,0:T(8,128)S(1)} copy-done((f32[128,256]{1,0:T(8,128)S(1)}, f32[128,256]{1,0:T(8,128)}, u32[]{:S(2)}) %copy-start.3) | copy-done | bytes 131096
  5.4 0.0 copy-start.4
  5.4 0.7 %copy-done.4 = s32[1,2,2,8]{3,2,1,0:T(2,128)S(1)} copy-done((s32[1,2,2,8]{3,2,1,0:T(2,128)S(1)}, s32[1,2,2,8]{3,2,1,0:T(2,128)}, u32[]{:S(2)}) %copy-start.4) | copy-done | bytes 152
  6.0 0.0 copy-start.5
  6.0 0.7 copy-done.5
  6.7 0.0 copy-start.6
  6.7 0.7 copy-done.6
  7.4 0.0 copy-start.7
  7.4 0.7 copy-done.7
  8.0 57.0 %schur.1 = f32[128,256]{1,0:T(8,128)S(1)} custom-call(s32[1,2]{1,0:T(1,128)S(1)} %copy-done.5, s32[1,2,2,8]{3,2,1,0:T(2,128)S(1)} %copy-done.4, s32[1,2]{1,0:T(1,128)S(1)} %copy-done.6, s32[1,2]{1,0:T(1,128)S(1)} %copy-done.7, bf16[1,1,512,1024]{3,2,1,0:T(8,128)(2,1)S(1)} %copy-done.1, bf16[1,2,1024,1024]{3,2,1,0:T(8,128)(2,1)S(1)} %copy-done, ...), custom_call_target="tpu_custom_call" | custom-call | tf_op jit(solution)/shard_map/schur/pallas_call | solution.py:434
  65.0 0.7 %copy.10 = f32[128,256]{1,0:T(8,128)} copy(f32[128,256]{1,0:T(8,128)S(1)} %schur.1) | data formatting | bytes 262144
Async XLA Ops:
  0.0 2.2 %copy-start = (bf16[1,2,1024,1024]{3,2,1,0:T(8,128)(2,1)S(1)}, bf16[1,2,1024,1024]{3,2,1,0:T(8,128)(2,1)}, u32[]{:S(2)}) copy-start(bf16[1,2,1024,1024]{3,2,1,0:T(8,128)(2,1)} %inverse_ref.1) | copy-start | bytes 12582916
  2.2 1.2 %copy-start.1 = (bf16[1,1,512,1024]{3,2,1,0:T(8,128)(2,1)S(1)}, bf16[1,1,512,1024]{3,2,1,0:T(8,128)(2,1)}, u32[]{:S(2)}) copy-start(bf16[1,1,512,1024]{3,2,1,0:T(8,128)(2,1)} %store_ref.1) | copy-start | bytes 3145732
  3.4 1.0 %copy-start.2 = (bf16[1,2,1024,128]{3,2,1,0:T(8,128)(2,1)S(1)}, bf16[1,2,1024,128]{3,2,1,0:T(8,128)(2,1)}, u32[]{:S(2)}) copy-start(bf16[1,2,1024,128]{3,2,1,0:T(8,128)(2,1)} %face_ref.1) | copy-start | bytes 1572868
  4.5 0.9 %copy-start.3 = (f32[128,256]{1,0:T(8,128)S(1)}, f32[128,256]{1,0:T(8,128)}, u32[]{:S(2)}) copy-start(f32[128,256]{1,0:T(8,128)} %iface_ref.1) | copy-start | bytes 393220
  5.4 0.7 %copy-start.4 = (s32[1,2,2,8]{3,2,1,0:T(2,128)S(1)}, s32[1,2,2,8]{3,2,1,0:T(2,128)}, u32[]{:S(2)}) copy-start(s32[1,2,2,8]{3,2,1,0:T(2,128)} %map_ref.1) | copy-start | bytes 388
  6.0 0.7 copy-start.5
  6.7 0.7 copy-start.6
  7.4 0.7 copy-start.7

commit v2 on v1

--- a/solution.py
+++ b/solution.py
@@ -16,21 +16,26 @@
 
 
 def kernel(
-    owner_ref,
-    map_ref,
-    offset_ref,
-    count_ref,
+    owner_hbm,
+    map_hbm,
+    offset_hbm,
+    count_hbm,
     store_ref,
     inverse_ref,
     face_ref,
     iface_ref,
     out_ref,
+    owner_ref,
+    map_ref,
+    offset_ref,
+    count_ref,
     st,
     inv,
     face,
     iface,
     r1_first,
     r1_second,
+    so,
     s2,
     r2,
     m2,
@@ -43,11 +48,15 @@
     band,
     nb,
     hs,
+    low,
     hf,
     pmat,
+    away,
     late,
     cross,
     load_sem,
+    s0_send,
+    s0_recv,
     s1_send,
     s1_recv,
     s2_send,
@@ -92,14 +101,11 @@
 
     partners = [device(x, zh, zl, y, oc)]
     for h in range(2):
-        for core in (c, oc):
-            partners.append(device(x, zh, zl, first_partner[h], core))
+        partners.append(device(x, zh, zl, first_partner[h], c))
     for a in range(4):
         for b in range(4):
             if a or b:
                 partners.append(device(flip(x, a), zh, flip(zl, b), y, c))
-    for a in range(1, 4):
-        partners.append(device(flip(x, a), zh, zl, y, oc))
     before, after = lax.rem(ifc + 31, 32), lax.rem(ifc + 1, 32)
     partners.append((sub, before))
     partners.append((sub, after))
@@ -109,6 +115,18 @@
     for partner in partners:
         pl.semaphore_signal(barrier, inc=1, device_id=partner, device_id_type=MESH)
 
+    scalar_loads = []
+    for at, (src, dst) in enumerate(
+        (
+            (owner_hbm, owner_ref),
+            (map_hbm, map_ref),
+            (offset_hbm, offset_ref),
+            (count_hbm, count_ref),
+        )
+    ):
+        cp = pltpu.make_async_copy(src, dst, load_sem.at[12 + at])
+        cp.start()
+        scalar_loads.append(cp)
     loads = []
     face_load = pltpu.make_async_copy(face_ref.at[0], face, load_sem.at[0])
     face_load.start()
@@ -132,68 +150,60 @@
     iface_load = pltpu.make_async_copy(iface_ref, iface, load_sem.at[n])
     iface_load.start()
 
-    face_load.wait()
-    row_at = lax.broadcasted_iota(jnp.int32, (256, 128), 0)
-    col_at = lax.broadcasted_iota(jnp.int32, (256, 128), 1)
-    for l in range(2):
-        start = offset_ref[0, l] - (ifc * 128 - 64)
-        here = jnp.logical_and(row_at == col_at + start, col_at < count_ref[0, l])
-        place = jnp.where(here, 1.0, 0.0).astype(BF16)
-        placed[l] = lax.dot_general(
-            place, face[l], NT_DIMS, preferred_element_type=F32
-        ).astype(BF16)
-    for l in range(2):
-        inv_loads[l].wait()
-
-        def columns(i, _):
-            at = pl.ds(aligned(i * 256, 256), 256)
-            gband[l, :, at] = jnp.dot(
-                placed[l], inv[l, :, at], preferred_element_type=F32
-            )
+    def place_rows():
+        face_load.wait()
+        row_at = lax.broadcasted_iota(jnp.int32, (256, 128), 0)
+        col_at = lax.broadcasted_iota(jnp.int32, (256, 128), 1)
+        for l in range(2):
+            start = offset_ref[0, l] - (ifc * 128 - 64)
+            here = jnp.logical_and(row_at == col_at + start, col_at < count_ref[0, l])
+            place = jnp.where(here, 1.0, 0.0).astype(BF16)
+            placed[l] = lax.dot_general(
+                place, face[l], NT_DIMS, preferred_element_type=F32
+            ).astype(BF16)
+
+    def apply_inverse():
+        for l in range(2):
+            inv_loads[l].wait()
+
+            def columns(i, _):
+                at = pl.ds(aligned(i * 256, 256), 256)
+                gband[l, :, at] = jnp.dot(
+                    placed[l], inv[l, :, at], preferred_element_type=F32
+                )
+                return 0
+
+            lax.fori_loop(0, 4, columns, 0)
+
+    def fold_tiles():
+        def fold(r, _):
+            rows = pl.ds(aligned(r * 64, 64), 64)
+            for k in range(2):
+                for t in range(4):
+                    acc = jnp.zeros((64, 128), F32)
+                    for l in range(2):
+                        for i in range(8):
+                            weight = jnp.where(map_ref[0, l, k, i] == t, 1.0, 0.0)
+                            acc = acc + weight * gband[l, rows, i * 128 : (i + 1) * 128]
+                    at = k * 512 + t * 128
+                    band[rows, at : at + 128] = acc
             return 0
 
-        lax.fori_loop(0, 4, columns, 0)
-
-    def fold(r, _):
-        rows = pl.ds(aligned(r * 64, 64), 64)
-        for k in range(2):
-            for t in range(4):
-                acc = jnp.zeros((64, 128), F32)
-                for l in range(2):
-                    for i in range(8):
-                        weight = jnp.where(map_ref[0, l, k, i] == t, 1.0, 0.0)
-                        acc = acc + weight * gband[l, rows, i * 128 : (i + 1) * 128]
-                at = k * 512 + t * 128
-                band[rows, at : at + 128] = acc
-        return 0
-
-    lax.fori_loop(0, 4, fold, 0)
+        lax.fori_loop(0, 4, fold, 0)
 
     for cp in loads:
         cp.wait()
     steps = ((1 - zh), zh)
-    for n in range(2):
-        for h in range(2):
-            rows = pl.ds(aligned(h * 256 + half[h] * 128, 128), 128)
-            r1[n][h, 0] = st[steps[n], :, c, rows, :]
+    def kept(h):
+        return pl.ds(aligned(h * 256 + half[h] * 128, 128), 128)
+
+    def given(h):
+        return pl.ds(aligned(h * 256 + (1 - half[h]) * 128, 128), 128)
+
+    def own_blocks(n):
+        for h in range(2):
+            r1[n][h, 0] = st[steps[n], :, c, kept(h), :]
             r1[n][h, 4] = jnp.zeros((2, 128, 128), BF16)
-
-    picks = []
-    for h in range(2):
-        row = []
-        for k in range(2):
-            o = owner_ref[0, k]
-            pick = jnp.int32(4)
-            sources = (
-                zl * 8 + y * 2 + c,
-                zl * 8 + y * 2 + oc,
-                zl * 8 + first_partner[h] * 2 + c,
-                zl * 8 + first_partner[h] * 2 + oc,
-            )
-            for at, source in enumerate(sources):
-                pick = jnp.where(o == source, at, pick)
-            row.append(pick)
-        picks.append(row)
 
     started = []
 
@@ -210,38 +220,71 @@
         started.append(cp)
         return cp
 
+    got = []
+
+    def arrive(cps):
+        for cp in cps:
+            cp.wait_recv()
+            got.append(cp)
+
     pl.semaphore_wait(barrier, len(partners))
 
+    def to_other_core(n):
+        out = []
+        for h in range(2):
+            out.append(
+                send(
+                    st.at[steps[n], :, oc, given(h), :],
+                    so.at[n, h],
+                    s0_send.at[n, h],
+                    s0_recv.at[n, h],
+                    device(x, zh, zl, y, oc),
+                )
+            )
+        return out
+
     def stage1(n):
-        cps = []
-        for h in range(2):
-            rows = pl.ds(aligned(h * 256 + (1 - half[h]) * 128, 128), 128)
-            for d, core in enumerate((c, oc)):
-                cps.append(
-                    send(
-                        st.at[steps[n], :, core, rows, :],
-                        r1[n].at[h, 2 + d],
-                        s1_send.at[n, h, d],
-                        s1_recv.at[n, h, d],
-                        device(x, zh, zl, first_partner[h], core),
-                    )
-                )
-            rows = pl.ds(aligned(h * 256 + half[h] * 128, 128), 128)
-            cps.append(
-                send(
-                    st.at[steps[n], :, oc, rows, :],
+        out = []
+        for h in range(2):
+            out.append(
+                send(
+                    st.at[steps[n], :, c, given(h), :],
+                    r1[n].at[h, 2],
+                    s1_send.at[n, h, 0],
+                    s1_recv.at[n, h, 0],
+                    device(x, zh, zl, first_partner[h], c),
+                )
+            )
+        return out
+
+    def stage1_rest(n, cps):
+        out = []
+        arrive(cps)
+        for h in range(2):
+            out.append(
+                send(
+                    so.at[n, h],
+                    r1[n].at[h, 3],
+                    s1_send.at[n, h, 1],
+                    s1_recv.at[n, h, 1],
+                    device(x, zh, zl, first_partner[h], c),
+                )
+            )
+        for h in range(2):
+            out.append(
+                send(
+                    st.at[steps[n], :, oc, kept(h), :],
                     r1[n].at[h, 1],
                     s1_send.at[n, h, 2],
                     s1_recv.at[n, h, 2],
                     device(x, zh, zl, y, oc),
                 )
             )
-        return cps
+        return out
 
     def stage2(n, cps):
         out = []
-        for cp in cps:
-            cp.wait_recv()
+        arrive(cps)
         for h in range(2):
             rows = pl.ds(aligned((1 - quarter[h]) * 64, 64), 64)
             for k in range(2):
@@ -259,8 +302,7 @@
 
     def stage3(n, cps):
         out = []
-        for cp in cps:
-            cp.wait_recv()
+        arrive(cps)
         for h in range(2):
             rows = pl.ds(aligned(quarter[h] * 64, 64), 64)
             for k in range(2):
@@ -282,8 +324,7 @@
 
     def stage4(n, cps):
         out = []
-        for cp in cps:
-            cp.wait_recv()
+        arrive(cps)
         rows = pl.ds(aligned(zl * 16, 16), 16)
         m3[n] = m2[n, :, :, rows, :] + r3[n, 1] + r3[n, 2] + r3[n, 3]
         for a in range(4):
@@ -303,8 +344,7 @@
 
     def stage5(n, cps):
         out = []
-        for cp in cps:
-            cp.wait_recv()
+        arrive(cps)
         for h in range(2):
             rows = pl.ds(aligned(h * 256 + half[h] * 128 + quarter[h] * 64, 64), 64)
             out.append(
@@ -321,8 +361,7 @@
 
     def stage6(n, cps):
         out = []
-        for cp in cps:
-            cp.wait_recv()
+        arrive(cps)
         for h in range(2):
             rows = pl.ds(aligned(h * 256 + half[h] * 128, 128), 128)
             out.append(
@@ -337,66 +376,106 @@
         return out
 
     def product(n, cps):
-        for cp in cps:
-            cp.wait_recv()
+        arrive(cps)
         total = jnp.zeros((256, 128), F32)
         for at in range(4):
             total = total + jnp.dot(hf[at], bmat[n, at], preferred_element_type=F32)
+        total = total + jnp.dot(hf[4], bmat[n, x], preferred_element_type=F32)
         pmat[n] = total
 
+    a0 = to_other_core(0)
     a1 = stage1(0)
+    a1 += stage1_rest(0, a0)
+    own_blocks(0)
+    for cp in scalar_loads:
+        cp.wait()
+    picks = []
+    for h in range(2):
+        row = []
+        for k in range(2):
+            o = owner_ref[0, k]
+            pick = jnp.int32(4)
+            sources = (
+                zl * 8 + y * 2 + c,
+                zl * 8 + y * 2 + oc,
+                zl * 8 + first_partner[h] * 2 + c,
+                zl * 8 + first_partner[h] * 2 + oc,
+            )
+            for at, source in enumerate(sources):
+                pick = jnp.where(o == source, at, pick)
+            row.append(pick)
+        picks.append(row)
+
+    place_rows()
+    apply_inverse()
+    a2 = stage2(0, a1)
+    b0 = to_other_core(1)
+    b1 = stage1(1)
+    b1 += stage1_rest(1, b0)
+    own_blocks(1)
+    fold_tiles()
+    a3 = stage3(0, a2)
     nb_cps = [
         send(band.at[0:64], nb.at[1], nb_send.at[0], nb_recv.at[0], (sub, before)),
         send(band.at[192:256], nb.at[0], nb_send.at[1], nb_recv.at[1], (sub, after)),
     ]
-    b1 = stage1(1)
-    a2 = stage2(0, a1)
-
-    for cp in nb_cps:
-        cp.wait_recv()
+    b2 = stage2(1, b1)
+    a4 = stage4(0, a3)
+    b3 = stage3(1, b2)
+
+    arrive(nb_cps)
     for k in range(2):
         at = slice(k * 512, (k + 1) * 512)
-        hs[k, 0:64] = (band[64:128, at] + nb[0, :, at]).astype(BF16)
-        hs[k, 64:128] = (band[128:192, at] + nb[1, :, at]).astype(BF16)
+        for part in range(2):
+            rows = slice(part * 64, (part + 1) * 64)
+            full = band[64 + part * 64 : 128 + part * 64, at] + nb[part, :, at]
+            high = full.astype(BF16)
+            hs[k, rows] = high
+            low[k, rows] = (full - high.astype(F32)).astype(BF16)
     own_rows = pl.ds(aligned(c * 128, 128), 128)
     h_cps = []
-    for a in range(4):
-        for d, core in enumerate((c, oc)):
-            if a or d:
-                h_cps.append(
-                    send(
-                        hs.at[flip(x, a) // 2],
-                        hf.at[x, own_rows, :],
-                        h_send.at[a, d],
-                        h_recv.at[a, d],
-                        device(flip(x, a), zh, zl, y, core),
-                    )
-                )
+    for a in range(1, 4):
+        h_cps.append(
+            send(
+                hs.at[flip(x, a) // 2],
+                hf.at[x, own_rows, :],
+                h_send.at[a],
+                h_recv.at[a],
+                device(flip(x, a), zh, zl, y, c),
+            )
+        )
     hf[x, own_rows, :] = hs[x // 2]
-
-    b2 = stage2(1, b1)
-    a3 = stage3(0, a2)
-    b3 = stage3(1, b2)
-    a4 = stage4(0, a3)
+    hf[4, own_rows, :] = low[x // 2]
+
     b4 = stage4(1, b3)
     a5 = stage5(0, a4)
+    a6 = stage6(0, a5)
     b5 = stage5(1, b4)
-    a6 = stage6(0, a5)
-    b6 = stage6(1, b5)
-    for cp in h_cps:
-        cp.wait_recv()
+    arrive(h_cps)
+    h_cps = [
+        send(
+            hf.at[:, own_rows, :],
+            hf.at[:, own_rows, :],
+            h_send.at[0],
+            h_recv.at[0],
+            device(x, zh, zl, y, oc),
+        )
+    ]
+    arrive(h_cps)
     product(0, a6)
+    away[...] = pmat[0].astype(BF16)
     late_cps = []
     for d, core in enumerate((c, oc)):
         late_cps.append(
             send(
-                pmat.at[0, pl.ds(aligned(core * 128, 128), 128), :],
+                away.at[pl.ds(aligned(core * 128, 128), 128), :],
                 late.at[d],
                 late_send.at[d],
                 late_recv.at[d],
                 device(x, 1 - zh, zl, y, core),
             )
         )
+    b6 = stage6(1, b5)
     product(1, b6)
     late_cps.append(
         send(
@@ -408,12 +487,11 @@
         )
     )
     iface_load.wait()
-    for cp in late_cps:
-        cp.wait_recv()
+    arrive(late_cps)
     own = pl.ds(aligned(c * 128, 128), 128)
     other = pl.ds(aligned(oc * 128, 128), 128)
-    out_ref[:, own] = iface[:, own] - (pmat[1, own, :] + late[0])
-    out_ref[:, other] = iface[:, other] - (cross[...] + late[1])
+    out_ref[:, own] = iface[:, own] - (pmat[1, own, :] + late[0].astype(F32))
+    out_ref[:, other] = iface[:, other] - (cross[...] + late[1].astype(F32))
     for cp in started:
         cp.wait_send()
 
@@ -428,21 +506,25 @@
     row_count,
     interface_block,
 ):
-    smem = pl.BlockSpec(memory_space=pltpu.SMEM)
-    anywhere = pl.BlockSpec(memory_space=pl.ANY)
+    hbm = pl.BlockSpec(memory_space=pltpu.HBM)
     dma = pltpu.SemaphoreType.DMA
     return pl.pallas_call(
         kernel,
         out_shape=jax.ShapeDtypeStruct((128, 256), F32),
-        in_specs=[smem] * 4 + [anywhere] * 4,
+        in_specs=[hbm] * 8,
         out_specs=pl.BlockSpec(memory_space=pltpu.VMEM),
         scratch_shapes=[
+            pltpu.SMEM((1, 2), jnp.int32),
+            pltpu.SMEM((1, 2, 2, 8), jnp.int32),
+            pltpu.SMEM((1, 2), jnp.int32),
+            pltpu.SMEM((1, 2), jnp.int32),
             pltpu.VMEM((2, 2, 2, 512, 128), BF16),
             pltpu.VMEM((2, 1024, 1024), BF16),
             pltpu.VMEM((2, 1024, 128), BF16),
             pltpu.VMEM((128, 256), F32),
             pltpu.VMEM((2, 5, 2, 128, 128), BF16),
             pltpu.VMEM((2, 5, 2, 128, 128), BF16),
+            pltpu.VMEM((2, 2, 2, 128, 128), BF16),
             pltpu.VMEM((2, 2, 4, 64, 128), BF16),
             pltpu.VMEM((2, 2, 4, 64, 128), BF16),
             pltpu.VMEM((2, 2, 4, 64, 128), BF16),
@@ -455,11 +537,15 @@
             pltpu.VMEM((256, 1024), F32),
             pltpu.VMEM((2, 64, 1024), F32),
             pltpu.VMEM((2, 128, 512), BF16),
-            pltpu.VMEM((4, 256, 512), BF16),
+            pltpu.VMEM((2, 128, 512), BF16),
+            pltpu.VMEM((5, 256, 512), BF16),
             pltpu.VMEM((2, 256, 128), F32),
-            pltpu.VMEM((2, 128, 128), F32),
+            pltpu.VMEM((256, 128), BF16),
+            pltpu.VMEM((2, 128, 128), BF16),
             pltpu.VMEM((128, 128), F32),
-            dma((12,)),
+            dma((16,)),
+            dma((2, 2)),
+            dma((2, 2)),
             dma((2, 2, 3)),
             dma((2, 2, 3)),
             dma((2, 2)),
@@ -474,13 +560,13 @@
             dma((2, 2)),
             dma((2,)),
             dma((2,)),
-            dma((4, 2)),
-            dma((4, 2)),
+            dma((4,)),
+            dma((4,)),
             dma((3,)),
             dma((3,)),
         ],
         compiler_params=pltpu.CompilerParams(
-            collective_id=0, has_side_effects=True, vmem_limit_bytes=40 * 1024 * 1024
+            collective_id=0, has_side_effects=True, vmem_limit_bytes=60 * 1024 * 1024
         ),
         name="schur",
     )(

time: 65.9 us -> 53.1 us (0.81)
  local copies, waits for them, and re-layouts: 8.66 us -> 1.57 us
  Pallas kernels: 57 us -> 51.4 us
    unnamed x17 -> x1, local copies, waits for them, and re-layouts: 8.66 us -> 1.57 us
    pallas_call x1, Pallas kernels: 57 us -> 51.4 us  [per_device(): pl.pallas_call(kernel, out_shape=jax.ShapeDtypeStruct((128, 256), F32), i...]
where the time goes in v2:
time: 53.1 us; the launch traced here: 53 us
  Pallas kernels  51.4 us (97%)
  local copies, waits for them, and re-layouts  1.57 us (3%)
    pallas_call x1, Pallas kernels, per_device(): pl.pallas_call(kernel, out_shape=jax.ShapeDtypeStruct((128, 256), F32), i...  51.4 us
    unnamed x1, local copies, waits for them, and re-layouts  1.57 us

profile of v2, /device:TPU:1, one launch (start us, length us, event | category | flops | bytes accessed | tf_op | source)
XLA Modules:
  0.0 53.0 jit_solution(16094864679830635586)
XLA Ops:
  0.0 51.4 %schur.1 = f32[128,256]{1,0:T(8,128)} custom-call(s32[1,2]{1,0:T(1,128)} %owner_hbm.1, s32[1,2,2,8]{3,2,1,0:T(2,128)} %map_hbm.1, s32[1,2]{1,0:T(1,128)} %offset_hbm.1, s32[1,2]{1,0:T(1,128)} %count_hbm.1, bf16[1,1,512,1024]{3,2,1,0:T(8,128)(2,1)} %store_ref.1, bf16[1,2,1024,1024]{3,2,1,0:T(8,128)(2,1)} %inverse_ref.1, bf16[1,2,1024,128]{3,2,1,0:T(8,128)(2,1)} %face_ref.1, ...), custom_call_target="tpu_custom_call" | custom-call | tf_op jit(solution)/shard_map/schur/pallas_call | solution.py:511
  51.4 1.6 %copy.10 = f32[128,256]{1,0:T(8,128)} copy(f32[128,256]{1,0:T(8,128)} %schur.1) | data formatting | bytes 262144

commit v3 on v2

--- a/solution.py
+++ b/solution.py
@@ -52,6 +52,7 @@
     hf,
     pmat,
     away,
+    away_sum,
     late,
     cross,
     load_sem,
@@ -109,12 +110,28 @@
     before, after = lax.rem(ifc + 31, 32), lax.rem(ifc + 1, 32)
     partners.append((sub, before))
     partners.append((sub, after))
-    for core in (c, oc):
-        partners.append(device(x, 1 - zh, zl, y, core))
+    partners.append(device(x, 1 - zh, zl, y, c))
+    steps = ((1 - zh), zh)
+    strips = ([], [])
+
+    def load_strips(n):
+        for xh in range(2):
+            for cc in range(2):
+                at = aligned(xh * 512 + steps[n] * 256 + cc * 128, 128)
+                cp = pltpu.make_async_copy(
+                    store_ref.at[0, 0, :, pl.ds(at, 128)],
+                    st.at[n, xh, cc],
+                    load_sem.at[n * 4 + xh * 2 + cc],
+                )
+                cp.start()
+                strips[n].append(cp)
+
+    load_strips(0)
     barrier = pltpu.get_barrier_semaphore()
     for partner in partners:
         pl.semaphore_signal(barrier, inc=1, device_id=partner, device_id_type=MESH)
 
+    load_strips(1)
     scalar_loads = []
     for at, (src, dst) in enumerate(
         (
@@ -124,30 +141,17 @@
             (count_hbm, count_ref),
         )
     ):
-        cp = pltpu.make_async_copy(src, dst, load_sem.at[12 + at])
+        cp = pltpu.make_async_copy(src, dst, load_sem.at[8 + at])
         cp.start()
         scalar_loads.append(cp)
-    loads = []
-    face_load = pltpu.make_async_copy(face_ref.at[0], face, load_sem.at[0])
+    face_load = pltpu.make_async_copy(face_ref.at[0], face, load_sem.at[12])
     face_load.start()
     inv_loads = []
     for l in range(2):
-        cp = pltpu.make_async_copy(inverse_ref.at[0, l], inv.at[l], load_sem.at[1 + l])
+        cp = pltpu.make_async_copy(inverse_ref.at[0, l], inv.at[l], load_sem.at[13 + l])
         cp.start()
         inv_loads.append(cp)
-    n = 3
-    for j in range(2):
-        for xh in range(2):
-            for cc in range(2):
-                cp = pltpu.make_async_copy(
-                    store_ref.at[0, 0, :, pl.ds(xh * 512 + j * 256 + cc * 128, 128)],
-                    st.at[j, xh, cc],
-                    load_sem.at[n],
-                )
-                cp.start()
-                loads.append(cp)
-                n += 1
-    iface_load = pltpu.make_async_copy(iface_ref, iface, load_sem.at[n])
+    iface_load = pltpu.make_async_copy(iface_ref, iface, load_sem.at[15])
     iface_load.start()
 
     def place_rows():
@@ -191,9 +195,6 @@
 
         lax.fori_loop(0, 4, fold, 0)
 
-    for cp in loads:
-        cp.wait()
-    steps = ((1 - zh), zh)
     def kept(h):
         return pl.ds(aligned(h * 256 + half[h] * 128, 128), 128)
 
@@ -202,13 +203,18 @@
 
     def own_blocks(n):
         for h in range(2):
-            r1[n][h, 0] = st[steps[n], :, c, kept(h), :]
+            r1[n][h, 0] = st[n, :, c, kept(h), :]
             r1[n][h, 4] = jnp.zeros((2, 128, 128), BF16)
 
     started = []
 
-    def send(src, dst, send_sem, recv_sem, to):
-        cp = pltpu.make_async_remote_copy(
+    mid = (zl // 2 + zl) % 2
+
+    def home_rows(home):
+        return pl.ds(aligned((home - 1) * 32, 32), 32)
+
+    def remote(src, dst, send_sem, recv_sem, to):
+        return pltpu.make_async_remote_copy(
             src_ref=src,
             dst_ref=dst,
             send_sem=send_sem,
@@ -216,6 +222,9 @@
             device_id=to,
             device_id_type=MESH,
         )
+
+    def send(src, dst, send_sem, recv_sem, to):
+        cp = remote(src, dst, send_sem, recv_sem, to)
         cp.start()
         started.append(cp)
         return cp
@@ -231,10 +240,12 @@
 
     def to_other_core(n):
         out = []
+        for cp in strips[n]:
+            cp.wait()
         for h in range(2):
             out.append(
                 send(
-                    st.at[steps[n], :, oc, given(h), :],
+                    st.at[n, :, oc, given(h), :],
                     so.at[n, h],
                     s0_send.at[n, h],
                     s0_recv.at[n, h],
@@ -248,7 +259,7 @@
         for h in range(2):
             out.append(
                 send(
-                    st.at[steps[n], :, c, given(h), :],
+                    st.at[n, :, c, given(h), :],
                     r1[n].at[h, 2],
                     s1_send.at[n, h, 0],
                     s1_recv.at[n, h, 0],
@@ -273,7 +284,7 @@
         for h in range(2):
             out.append(
                 send(
-                    st.at[steps[n], :, oc, kept(h), :],
+                    st.at[n, :, oc, kept(h), :],
                     r1[n].at[h, 1],
                     s1_send.at[n, h, 2],
                     s1_recv.at[n, h, 2],
@@ -301,7 +312,6 @@
         return out
 
     def stage3(n, cps):
-        out = []
         arrive(cps)
         for h in range(2):
             rows = pl.ds(aligned(quarter[h] * 64, 64), 64)
@@ -309,42 +319,75 @@
                 m2[n, h, 2 * k : 2 * k + 2] = (
                     r1[n][h, picks[h][k], :, rows, :] + r2[n, h, 2 * k : 2 * k + 2]
                 )
-        for d in range(1, 4):
-            to = flip(zl, d)
-            out.append(
-                send(
-                    m2.at[n, :, :, pl.ds(aligned(to * 16, 16), 16), :],
-                    r3.at[n, d],
-                    s3_send.at[n, d],
-                    s3_recv.at[n, d],
-                    device(x, zh, to, y, c),
-                )
-            )
-        return out
-
-    def stage4(n, cps):
+        a_home, b_home = 1 + zl % 2, 2 - zl % 2
+        send(
+            m2.at[n, :, :, home_rows(a_home), :],
+            r3.at[n, mid],
+            s3_send.at[n, 0],
+            s3_recv.at[n, mid],
+            device(x, zh, a_home, y, c),
+        )
+
+        @pl.when(mid == 0)
+        def _():
+            remote(
+                m2.at[n, :, :, home_rows(b_home), :],
+                r3.at[n, 2],
+                s3_send.at[n, 1],
+                s3_recv.at[n, 2],
+                device(x, zh, b_home, y, c),
+            ).start()
+
+    def spread(n, a, b):
+        return remote(
+            m3.at[n, :, flip(x, a)],
+            r4.at[n, x, :, home_rows(zl), :],
+            s4_send.at[n, a, b],
+            s4_recv.at[n, a, zl - 1],
+            device(flip(x, a), zh, flip(zl, b), y, c),
+        )
+
+    def stage4(n):
+        @pl.when(mid == 1)
+        def _():
+            for slot in range(3):
+                remote(
+                    r3.at[n, slot],
+                    r3.at[n, slot],
+                    s3_send.at[n, 0],
+                    s3_recv.at[n, slot],
+                    device(x, zh, zl, y, oc),
+                ).wait_recv()
+            m3[n] = (
+                m2[n, :, :, home_rows(zl), :] + r3[n, 0] + r3[n, 1] + r3[n, 2]
+            )
+            for b in (1, 2, 3, 0):
+                for a in range(4):
+                    if a or b:
+                        spread(n, a, b).start()
+            r4[n, x, :, home_rows(zl), :] = m3[n, :, x]
+
+    def from_home(n, a, home):
+        rows = home_rows(home)
+        remote(
+            r4.at[n, flip(x, a), :, rows, :],
+            r4.at[n, flip(x, a), :, rows, :],
+            s4_send.at[n, 0, 0],
+            s4_recv.at[n, a, home - 1],
+            device(x, zh, zl, y, oc),
+        ).wait_recv()
+
+    def stage5(n):
+        from_home(n, 0, 1 + mid * (2 - zl))
+        for a in range(1, 4):
+            for home in (1, 2):
+                from_home(n, a, home)
+
+        @pl.when(mid == 0)
+        def _():
+            from_home(n, 0, 2)
+
         out = []
-        arrive(cps)
-        rows = pl.ds(aligned(zl * 16, 16), 16)
-        m3[n] = m2[n, :, :, rows, :] + r3[n, 1] + r3[n, 2] + r3[n, 3]
-        for a in range(4):
-            for b in range(4):
-                if a or b:
-                    out.append(
-                        send(
-                            m3.at[n, :, flip(x, a)],
-                            r4.at[n, x, :, rows, :],
-                            s4_send.at[n, a, b],
-                            s4_recv.at[n, a, b],
-                            device(flip(x, a), zh, flip(zl, b), y, c),
-                        )
-                    )
-        r4[n, x, :, rows, :] = m3[n, :, x]
-        return out
-
-    def stage5(n, cps):
-        out = []
-        arrive(cps)
         for h in range(2):
             rows = pl.ds(aligned(h * 256 + half[h] * 128 + quarter[h] * 64, 64), 64)
             out.append(
@@ -375,13 +418,13 @@
             )
         return out
 
-    def product(n, cps):
-        arrive(cps)
-        total = jnp.zeros((256, 128), F32)
+    def product(n, rows):
+        total = jnp.dot(hf[4, rows, :], bmat[n, x], preferred_element_type=F32)
         for at in range(4):
-            total = total + jnp.dot(hf[at], bmat[n, at], preferred_element_type=F32)
-        total = total + jnp.dot(hf[4], bmat[n, x], preferred_element_type=F32)
-        pmat[n] = total
+            total = total + jnp.dot(
+                hf[at, rows, :], bmat[n, at], preferred_element_type=F32
+            )
+        return total
 
     a0 = to_other_core(0)
     a1 = stage1(0)
@@ -414,15 +457,14 @@
     b1 += stage1_rest(1, b0)
     own_blocks(1)
     fold_tiles()
-    a3 = stage3(0, a2)
+    stage3(0, a2)
     nb_cps = [
         send(band.at[0:64], nb.at[1], nb_send.at[0], nb_recv.at[0], (sub, before)),
         send(band.at[192:256], nb.at[0], nb_send.at[1], nb_recv.at[1], (sub, after)),
     ]
     b2 = stage2(1, b1)
-    a4 = stage4(0, a3)
-    b3 = stage3(1, b2)
-
+    stage4(0)
+    stage3(1, b2)
     arrive(nb_cps)
     for k in range(2):
         at = slice(k * 512, (k + 1) * 512)
@@ -447,10 +489,9 @@
     hf[x, own_rows, :] = hs[x // 2]
     hf[4, own_rows, :] = low[x // 2]
 
-    b4 = stage4(1, b3)
-    a5 = stage5(0, a4)
+    stage4(1)
+    a5 = stage5(0)
     a6 = stage6(0, a5)
-    b5 = stage5(1, b4)
     arrive(h_cps)
     h_cps = [
         send(
@@ -461,39 +502,50 @@
             device(x, zh, zl, y, oc),
         )
     ]
+    b5 = stage5(1)
     arrive(h_cps)
-    product(0, a6)
-    away[...] = pmat[0].astype(BF16)
-    late_cps = []
-    for d, core in enumerate((c, oc)):
-        late_cps.append(
-            send(
-                away.at[pl.ds(aligned(core * 128, 128), 128), :],
-                late.at[d],
-                late_send.at[d],
-                late_recv.at[d],
-                device(x, 1 - zh, zl, y, core),
-            )
-        )
+    arrive(a6)
+    away[...] = product(0, slice(0, 256)).astype(BF16)
+    late_cps = [
+        send(away, late, late_send.at[0], late_recv.at[0], device(x, 1 - zh, zl, y, c))
+    ]
     b6 = stage6(1, b5)
-    product(1, b6)
-    late_cps.append(
-        send(
-            pmat.at[1, pl.ds(aligned(oc * 128, 128), 128), :],
-            cross,
-            late_send.at[2],
-            late_recv.at[2],
-            device(x, zh, zl, y, oc),
-        )
-    )
-    iface_load.wait()
-    arrive(late_cps)
+    arrive(b6)
     own = pl.ds(aligned(c * 128, 128), 128)
     other = pl.ds(aligned(oc * 128, 128), 128)
-    out_ref[:, own] = iface[:, own] - (pmat[1, own, :] + late[0].astype(F32))
-    out_ref[:, other] = iface[:, other] - (cross[...] + late[1].astype(F32))
+    both = product(1, slice(0, 256))
+    pmat[...] = both
+    arrive(late_cps)
+    away_sum[...] = pmat[other, :] + late[other, :].astype(F32)
+    late_cps = [
+        send(
+            away_sum, cross, late_send.at[1], late_recv.at[1], device(x, zh, zl, y, oc)
+        )
+    ]
+    iface_load.wait()
+    out_ref[:, own] = iface[:, own] - (pmat[own, :] + late[own, :].astype(F32))
+    arrive(late_cps)
+    out_ref[:, other] = iface[:, other] - cross[...]
     for cp in started:
         cp.wait_send()
+    for n in range(2):
+
+        @pl.when(mid == 0)
+        def _():
+            remote(
+                m2.at[n, :, :, home_rows(1), :],
+                r3.at[n, 2],
+                s3_send.at[n, 1],
+                s3_recv.at[n, 2],
+                device(x, zh, zl, y, oc),
+            ).wait_send()
+
+        @pl.when(mid == 1)
+        def _():
+            for a in range(4):
+                for b in range(4):
+                    if a or b:
+                        spread(n, a, b).wait_send()
 
 
 def per_device(
@@ -510,7 +562,7 @@
     dma = pltpu.SemaphoreType.DMA
     return pl.pallas_call(
         kernel,
-        out_shape=jax.ShapeDtypeStruct((128, 256), F32),
+        out_shape=pltpu.VMEM((128, 256), F32),
         in_specs=[hbm] * 8,
         out_specs=pl.BlockSpec(memory_space=pltpu.VMEM),
         scratch_shapes=[
@@ -528,8 +580,8 @@
             pltpu.VMEM((2, 2, 4, 64, 128), BF16),
             pltpu.VMEM((2, 2, 4, 64, 128), BF16),
             pltpu.VMEM((2, 2, 4, 64, 128), BF16),
-            pltpu.VMEM((2, 4, 2, 4, 16, 128), BF16),
-            pltpu.VMEM((2, 2, 4, 16, 128), BF16),
+            pltpu.VMEM((2, 3, 2, 4, 32, 128), BF16),
+            pltpu.VMEM((2, 2, 4, 32, 128), BF16),
             pltpu.VMEM((2, 4, 2, 64, 128), BF16),
             pltpu.VMEM((2, 4, 512, 128), BF16),
             pltpu.VMEM((2, 256, 1024), BF16),
@@ -539,9 +591,10 @@
             pltpu.VMEM((2, 128, 512), BF16),
             pltpu.VMEM((2, 128, 512), BF16),
             pltpu.VMEM((5, 256, 512), BF16),
-            pltpu.VMEM((2, 256, 128), F32),
+            pltpu.VMEM((256, 128), F32),
             pltpu.VMEM((256, 128), BF16),
-            pltpu.VMEM((2, 128, 128), BF16),
+            pltpu.VMEM((128, 128), F32),
+            pltpu.VMEM((256, 128), BF16),
             pltpu.VMEM((128, 128), F32),
             dma((16,)),
             dma((2, 2)),
@@ -550,10 +603,10 @@
             dma((2, 2, 3)),
             dma((2, 2)),
             dma((2, 2)),
-            dma((2, 4)),
-            dma((2, 4)),
+            dma((2, 2)),
+            dma((2, 3)),
             dma((2, 4, 4)),
-            dma((2, 4, 4)),
+            dma((2, 4, 2)),
             dma((2, 2)),
             dma((2, 2)),
             dma((2, 2)),
@@ -566,18 +619,23 @@
             dma((3,)),
         ],
         compiler_params=pltpu.CompilerParams(
-            collective_id=0, has_side_effects=True, vmem_limit_bytes=60 * 1024 * 1024
+            collective_id=0, has_side_effects=True, vmem_limit_bytes=40 * 1024 * 1024
         ),
         name="schur",
     )(
-        stretch_owner,
-        tile_map,
-        row_offset,
-        row_count,
-        stretch_store,
-        inverse_block,
-        face_coupling,
-        interface_block,
+        *(
+            pltpu.with_memory_space_constraint(operand, pltpu.HBM)
+            for operand in (
+                stretch_owner,
+                tile_map,
+                row_offset,
+                row_count,
+                stretch_store,
+                inverse_block,
+                face_coupling,
+                interface_block,
+            )
+        )
     )
 
 

time: 53.1 us -> 51.2 us (0.964)
  Pallas kernels: 51.4 us -> 50.4 us
  local copies, waits for them, and re-layouts: 1.57 us -> 0.66 us
    pallas_call x1, Pallas kernels: 51.4 us -> 50.4 us  [per_device(): pl.pallas_call(kernel, out_shape=pltpu.VMEM((128, 256), F32), in_specs=[h...]
    unnamed x1, local copies, waits for them, and re-layouts: 1.57 us -> 0.66 us
where the time goes in v3:
time: 51.2 us; the launch traced here: 51.1 us
  Pallas kernels  50.4 us (98%)
  local copies, waits for them, and re-layouts  0.66 us (1%)
    pallas_call x1, Pallas kernels, per_device(): pl.pallas_call(kernel, out_shape=pltpu.VMEM((128, 256), F32), in_specs=[h...  50.4 us

profile of v3, /device:TPU:1, one launch (start us, length us, event | category | flops | bytes accessed | tf_op | source)
XLA Modules:
  0.0 51.1 jit_solution(10760157864546968778)
XLA Ops:
  0.0 50.4 %schur.1 = f32[128,256]{1,0:T(8,128)S(1)} custom-call(s32[1,2]{1,0:T(1,128)} %owner_hbm.1, s32[1,2,2,8]{3,2,1,0:T(2,128)} %map_hbm.1, s32[1,2]{1,0:T(1,128)} %offset_hbm.1, s32[1,2]{1,0:T(1,128)} %count_hbm.1, bf16[1,1,512,1024]{3,2,1,0:T(8,128)(2,1)} %store_ref.1, bf16[1,2,1024,1024]{3,2,1,0:T(8,128)(2,1)} %inverse_ref.1, ...), custom_call_target="tpu_custom_call" | custom-call | tf_op jit(solution)/shard_map/schur/pallas_call | solution.py:563
  50.4 0.7 %copy.10 = f32[128,256]{1,0:T(8,128)} copy(f32[128,256]{1,0:T(8,128)S(1)} %schur.1) | data formatting | bytes 262144

commit v4 on v3

--- a/solution.py
+++ b/solution.py
@@ -76,6 +76,7 @@
     h_recv,
     late_send,
     late_recv,
+    ready,
 ):
     sub = lax.axis_index("sub")
     ifc = lax.axis_index("ifc")
@@ -110,7 +111,6 @@
     before, after = lax.rem(ifc + 31, 32), lax.rem(ifc + 1, 32)
     partners.append((sub, before))
     partners.append((sub, after))
-    partners.append(device(x, 1 - zh, zl, y, c))
     steps = ((1 - zh), zh)
     strips = ([], [])
 
@@ -179,21 +179,23 @@
 
             lax.fori_loop(0, 4, columns, 0)
 
-    def fold_tiles():
+    def fold_tiles(first, step):
         def fold(r, _):
-            rows = pl.ds(aligned(r * 64, 64), 64)
+            rows = pl.ds(aligned((first + r * step) * 64, 64), 64)
             for k in range(2):
+                accs = [jnp.zeros((64, 128), F32) for _ in range(4)]
+                for l in range(2):
+                    for i in range(8):
+                        block = gband[l, rows, i * 128 : (i + 1) * 128]
+                        tile = map_ref[0, l, k, i]
+                        for t in range(4):
+                            accs[t] = accs[t] + jnp.where(tile == t, 1.0, 0.0) * block
                 for t in range(4):
-                    acc = jnp.zeros((64, 128), F32)
-                    for l in range(2):
-                        for i in range(8):
-                            weight = jnp.where(map_ref[0, l, k, i] == t, 1.0, 0.0)
-                            acc = acc + weight * gband[l, rows, i * 128 : (i + 1) * 128]
                     at = k * 512 + t * 128
-                    band[rows, at : at + 128] = acc
+                    band[rows, at : at + 128] = accs[t]
             return 0
 
-        lax.fori_loop(0, 4, fold, 0)
+        lax.fori_loop(0, 2, fold, 0)
 
     def kept(h):
         return pl.ds(aligned(h * 256 + half[h] * 128, 128), 128)
@@ -236,7 +238,17 @@
             cp.wait_recv()
             got.append(cp)
 
-    pl.semaphore_wait(barrier, len(partners))
+    opposite = device(x, 1 - zh, zl, y, c)
+    pl.semaphore_wait(barrier, len(partners) + zh)
+
+    @pl.when(zh == 0)
+    def _():
+        pl.semaphore_signal(barrier, inc=1, device_id=opposite, device_id_type=MESH)
+
+    @pl.when(zh == 1)
+    def _():
+        pl.semaphore_signal(ready, inc=1, device_id=opposite, device_id_type=MESH)
+
 
     def to_other_core(n):
         out = []
@@ -456,8 +468,9 @@
     b1 = stage1(1)
     b1 += stage1_rest(1, b0)
     own_blocks(1)
-    fold_tiles()
     stage3(0, a2)
+    fold_tiles(0, 3)
+    fold_tiles(1, 1)
     nb_cps = [
         send(band.at[0:64], nb.at[1], nb_send.at[0], nb_recv.at[0], (sub, before)),
         send(band.at[192:256], nb.at[0], nb_send.at[1], nb_recv.at[1], (sub, after)),
@@ -489,8 +502,8 @@
     hf[x, own_rows, :] = hs[x // 2]
     hf[4, own_rows, :] = low[x // 2]
 
+    a5 = stage5(0)
     stage4(1)
-    a5 = stage5(0)
     a6 = stage6(0, a5)
     arrive(h_cps)
     h_cps = [
@@ -506,9 +519,12 @@
     arrive(h_cps)
     arrive(a6)
     away[...] = product(0, slice(0, 256)).astype(BF16)
-    late_cps = [
-        send(away, late, late_send.at[0], late_recv.at[0], device(x, 1 - zh, zl, y, c))
-    ]
+
+    @pl.when(zh == 0)
+    def _():
+        pl.semaphore_wait(ready, 1)
+
+    late_cps = [send(away, late, late_send.at[0], late_recv.at[0], opposite)]
     b6 = stage6(1, b5)
     arrive(b6)
     own = pl.ds(aligned(c * 128, 128), 128)
@@ -615,8 +631,9 @@
             dma((2,)),
             dma((4,)),
             dma((4,)),
-            dma((3,)),
-            dma((3,)),
+            dma((2,)),
+            dma((2,)),
+            pltpu.SemaphoreType.REGULAR,
         ],
         compiler_params=pltpu.CompilerParams(
             collective_id=0, has_side_effects=True, vmem_limit_bytes=40 * 1024 * 1024

time: 51.2 us -> 49.5 us (0.967)
  Pallas kernels: 50.4 us -> 48.6 us
    pallas_call x1, Pallas kernels: 50.4 us -> 48.6 us  [per_device(): pl.pallas_call(kernel, out_shape=pltpu.VMEM((128, 256), F32), in_specs=[h...]
where the time goes in v4:
time: 49.5 us; the launch traced here: 49.2 us
  Pallas kernels  48.6 us (98%)
  local copies, waits for them, and re-layouts  0.66 us (1%)
    pallas_call x1, Pallas kernels, per_device(): pl.pallas_call(kernel, out_shape=pltpu.VMEM((128, 256), F32), in_specs=[h...  48.6 us

profile of v4, /device:TPU:1, one launch (start us, length us, event | category | flops | bytes accessed | tf_op | source)
XLA Modules:
  0.0 49.2 jit_solution(15378917198334133805)
XLA Ops:
  0.0 48.6 %schur.1 = f32[128,256]{1,0:T(8,128)S(1)} custom-call(s32[1,2]{1,0:T(1,128)} %owner_hbm.1, s32[1,2,2,8]{3,2,1,0:T(2,128)} %map_hbm.1, s32[1,2]{1,0:T(1,128)} %offset_hbm.1, s32[1,2]{1,0:T(1,128)} %count_hbm.1, bf16[1,1,512,1024]{3,2,1,0:T(8,128)(2,1)} %store_ref.1, bf16[1,2,1024,1024]{3,2,1,0:T(8,128)(2,1)} %inverse_ref.1, ...), custom_call_target="tpu_custom_call" | custom-call | tf_op jit(solution)/shard_map/schur/pallas_call | solution.py:579
  48.6 0.7 %copy.10 = f32[128,256]{1,0:T(8,128)} copy(f32[128,256]{1,0:T(8,128)S(1)} %schur.1) | data formatting | bytes 262144

commit v5 on v4

--- a/solution.py
+++ b/solution.py
@@ -52,7 +52,6 @@
     hf,
     pmat,
     away,
-    away_sum,
     late,
     cross,
     load_sem,
@@ -105,12 +104,12 @@
     for h in range(2):
         partners.append(device(x, zh, zl, first_partner[h], c))
     for a in range(4):
-        for b in range(4):
+        for b in range(3):
             if a or b:
                 partners.append(device(flip(x, a), zh, flip(zl, b), y, c))
     before, after = lax.rem(ifc + 31, 32), lax.rem(ifc + 1, 32)
-    partners.append((sub, before))
-    partners.append((sub, after))
+    partners.append((sub, lax.rem(ifc + 31 + 2 * c, 32)))
+    mid = (zl // 2 + zl) % 2
     steps = ((1 - zh), zh)
     strips = ([], [])
 
@@ -130,6 +129,17 @@
     barrier = pltpu.get_barrier_semaphore()
     for partner in partners:
         pl.semaphore_signal(barrier, inc=1, device_id=partner, device_id_type=MESH)
+
+    @pl.when(mid == 1)
+    def _():
+        for a in range(4):
+            pl.semaphore_signal(
+                barrier,
+                inc=1,
+                device_id=device(flip(x, a), zh, 3 - zl, y, c),
+                device_id_type=MESH,
+            )
+
 
     load_strips(1)
     scalar_loads = []
@@ -210,8 +220,6 @@
 
     started = []
 
-    mid = (zl // 2 + zl) % 2
-
     def home_rows(home):
         return pl.ds(aligned((home - 1) * 32, 32), 32)
 
@@ -239,21 +247,23 @@
             got.append(cp)
 
     opposite = device(x, 1 - zh, zl, y, c)
-    pl.semaphore_wait(barrier, len(partners) + zh)
+    pl.semaphore_wait(barrier, len(partners) + 2 * zh + 4 * mid)
+
+    opposites = (opposite, device(x, 1 - zh, zl, y, oc))
 
     @pl.when(zh == 0)
     def _():
-        pl.semaphore_signal(barrier, inc=1, device_id=opposite, device_id_type=MESH)
+        for to in opposites:
+            pl.semaphore_signal(barrier, inc=1, device_id=to, device_id_type=MESH)
 
     @pl.when(zh == 1)
     def _():
-        pl.semaphore_signal(ready, inc=1, device_id=opposite, device_id_type=MESH)
+        for to in opposites:
+            pl.semaphore_signal(ready, inc=1, device_id=to, device_id_type=MESH)
 
 
     def to_other_core(n):
         out = []
-        for cp in strips[n]:
-            cp.wait()
         for h in range(2):
             out.append(
                 send(
@@ -268,6 +278,8 @@
 
     def stage1(n):
         out = []
+        for cp in strips[n]:
+            cp.wait()
         for h in range(2):
             out.append(
                 send(
@@ -373,8 +385,8 @@
             m3[n] = (
                 m2[n, :, :, home_rows(zl), :] + r3[n, 0] + r3[n, 1] + r3[n, 2]
             )
-            for b in (1, 2, 3, 0):
-                for a in range(4):
+            for b in (2, 3, 1, 0):
+                for a in (2, 1, 3, 0):
                     if a or b:
                         spread(n, a, b).start()
             r4[n, x, :, home_rows(zl), :] = m3[n, :, x]
@@ -438,8 +450,8 @@
             )
         return total
 
+    a1 = stage1(0)
     a0 = to_other_core(0)
-    a1 = stage1(0)
     a1 += stage1_rest(0, a0)
     own_blocks(0)
     for cp in scalar_loads:
@@ -464,8 +476,8 @@
     place_rows()
     apply_inverse()
     a2 = stage2(0, a1)
+    b1 = stage1(1)
     b0 = to_other_core(1)
-    b1 = stage1(1)
     b1 += stage1_rest(1, b0)
     own_blocks(1)
     stage3(0, a2)
@@ -518,30 +530,31 @@
     b5 = stage5(1)
     arrive(h_cps)
     arrive(a6)
-    away[...] = product(0, slice(0, 256)).astype(BF16)
-
     @pl.when(zh == 0)
     def _():
-        pl.semaphore_wait(ready, 1)
-
-    late_cps = [send(away, late, late_send.at[0], late_recv.at[0], opposite)]
+        pl.semaphore_wait(ready, 2)
+
+    late_cps = []
+    for d, core in enumerate((c, oc)):
+        rows = pl.ds(aligned(core * 128, 128), 128)
+        away[d] = product(0, rows).astype(BF16)
+        late_cps.append(
+            send(away.at[d], late.at[d], late_send.at[d], late_recv.at[d], opposites[d])
+        )
     b6 = stage6(1, b5)
     arrive(b6)
     own = pl.ds(aligned(c * 128, 128), 128)
     other = pl.ds(aligned(oc * 128, 128), 128)
-    both = product(1, slice(0, 256))
-    pmat[...] = both
+    pmat[...] = product(1, other)
+    late_cps.append(
+        send(pmat, cross, late_send.at[2], late_recv.at[2], device(x, zh, zl, y, oc))
+    )
+    mine = product(1, own)
+    iface_load.wait()
+    out_ref[:, own] = iface[:, own] - mine
     arrive(late_cps)
-    away_sum[...] = pmat[other, :] + late[other, :].astype(F32)
-    late_cps = [
-        send(
-            away_sum, cross, late_send.at[1], late_recv.at[1], device(x, zh, zl, y, oc)
-        )
-    ]
-    iface_load.wait()
-    out_ref[:, own] = iface[:, own] - (pmat[own, :] + late[own, :].astype(F32))
-    arrive(late_cps)
-    out_ref[:, other] = iface[:, other] - cross[...]
+    out_ref[:, own] = out_ref[:, own] - late[0].astype(F32)
+    out_ref[:, other] = iface[:, other] - (cross[...] + late[1].astype(F32))
     for cp in started:
         cp.wait_send()
     for n in range(2):
@@ -607,10 +620,9 @@
             pltpu.VMEM((2, 128, 512), BF16),
             pltpu.VMEM((2, 128, 512), BF16),
             pltpu.VMEM((5, 256, 512), BF16),
-            pltpu.VMEM((256, 128), F32),
-            pltpu.VMEM((256, 128), BF16),
             pltpu.VMEM((128, 128), F32),
-            pltpu.VMEM((256, 128), BF16),
+            pltpu.VMEM((2, 128, 128), BF16),
+            pltpu.VMEM((2, 128, 128), BF16),
             pltpu.VMEM((128, 128), F32),
             dma((16,)),
             dma((2, 2)),
@@ -631,8 +643,8 @@
             dma((2,)),
             dma((4,)),
             dma((4,)),
-            dma((2,)),
-            dma((2,)),
+            dma((3,)),
+            dma((3,)),
             pltpu.SemaphoreType.REGULAR,
         ],
         compiler_params=pltpu.CompilerParams(

time: 49.5 us -> 48.5 us (0.980)
  Pallas kernels: 48.6 us -> 47.8 us
    pallas_call x1, Pallas kernels: 48.6 us -> 47.8 us  [per_device(): pl.pallas_call(kernel, out_shape=pltpu.VMEM((128, 256), F32), in_specs=[h...]
where the time goes in v5:
time: 48.5 us
  Pallas kernels  47.8 us (99%)
  local copies, waits for them, and re-layouts  0.66 us (1%)
    pallas_call x1, Pallas kernels, per_device(): pl.pallas_call(kernel, out_shape=pltpu.VMEM((128, 256), F32), in_specs=[h...  47.8 us

profile of v5, /device:TPU:1, one launch (start us, length us, event | category | flops | bytes accessed | tf_op | source)
XLA Modules:
  0.0 48.5 jit_solution(5088234939735612055)
XLA Ops:
  0.0 47.8 %schur.1 = f32[128,256]{1,0:T(8,128)S(1)} custom-call(s32[1,2]{1,0:T(1,128)} %owner_hbm.1, s32[1,2,2,8]{3,2,1,0:T(2,128)} %map_hbm.1, s32[1,2]{1,0:T(1,128)} %offset_hbm.1, s32[1,2]{1,0:T(1,128)} %count_hbm.1, bf16[1,1,512,1024]{3,2,1,0:T(8,128)(2,1)} %store_ref.1, bf16[1,2,1024,1024]{3,2,1,0:T(8,128)(2,1)} %inverse_ref.1, ...), custom_call_target="tpu_custom_call" | custom-call | tf_op jit(solution)/shard_map/schur/pallas_call | solution.py:592
  47.8 0.7 %copy.10 = f32[128,256]{1,0:T(8,128)} copy(f32[128,256]{1,0:T(8,128)S(1)} %schur.1) | data formatting | bytes 262144

commit v6 on v5

--- a/solution.py
+++ b/solution.py
@@ -489,7 +489,6 @@
     ]
     b2 = stage2(1, b1)
     stage4(0)
-    stage3(1, b2)
     arrive(nb_cps)
     for k in range(2):
         at = slice(k * 512, (k + 1) * 512)
@@ -514,6 +513,7 @@
     hf[x, own_rows, :] = hs[x // 2]
     hf[4, own_rows, :] = low[x // 2]
 
+    stage3(1, b2)
     a5 = stage5(0)
     stage4(1)
     a6 = stage6(0, a5)

time: 48.5 us -> 48.5 us (level)
  no operation moved by 1% of the time
where the time goes in v6:
time: 48.5 us
  Pallas kernels  47.8 us (99%)
  local copies, waits for them, and re-layouts  0.66 us (1%)
    pallas_call x1, Pallas kernels, per_device(): pl.pallas_call(kernel, out_shape=pltpu.VMEM((128, 256), F32), in_specs=[h...  47.8 us

profile of v6, /device:TPU:1, one launch (start us, length us, event | category | flops | bytes accessed | tf_op | source)
XLA Modules:
  0.0 48.5 jit_solution(2722915332061265140)
XLA Ops:
  0.0 47.8 %schur.1 = f32[128,256]{1,0:T(8,128)S(1)} custom-call(s32[1,2]{1,0:T(1,128)} %owner_hbm.1, s32[1,2,2,8]{3,2,1,0:T(2,128)} %map_hbm.1, s32[1,2]{1,0:T(1,128)} %offset_hbm.1, s32[1,2]{1,0:T(1,128)} %count_hbm.1, bf16[1,1,512,1024]{3,2,1,0:T(8,128)(2,1)} %store_ref.1, bf16[1,2,1024,1024]{3,2,1,0:T(8,128)(2,1)} %inverse_ref.1, ...), custom_call_target="tpu_custom_call" | custom-call | tf_op jit(solution)/shard_map/schur/pallas_call | solution.py:592
  47.8 0.7 %copy.10 = f32[128,256]{1,0:T(8,128)} copy(f32[128,256]{1,0:T(8,128)S(1)} %schur.1) | data formatting | bytes 262144

commit v7 on v6

--- a/solution.py
+++ b/solution.py
@@ -513,20 +513,25 @@
     hf[x, own_rows, :] = hs[x // 2]
     hf[4, own_rows, :] = low[x // 2]
 
+    def share(at, slot):
+        return send(
+            hf.at[at, own_rows, :],
+            hf.at[at, own_rows, :],
+            h_send.at[slot],
+            h_recv.at[slot],
+            device(x, zh, zl, y, oc),
+        )
+
+    shared = [share(x, 0), share(4, 7)]
+
     stage3(1, b2)
     a5 = stage5(0)
     stage4(1)
     a6 = stage6(0, a5)
-    arrive(h_cps)
-    h_cps = [
-        send(
-            hf.at[:, own_rows, :],
-            hf.at[:, own_rows, :],
-            h_send.at[0],
-            h_recv.at[0],
-            device(x, zh, zl, y, oc),
-        )
-    ]
+    for a, cp in enumerate(h_cps, 1):
+        arrive([cp])
+        shared.append(share(flip(x, a), 3 + a))
+    h_cps = shared
     b5 = stage5(1)
     arrive(h_cps)
     arrive(a6)
@@ -641,8 +646,8 @@
             dma((2, 2)),
             dma((2,)),
             dma((2,)),
-            dma((4,)),
-            dma((4,)),
+            dma((8,)),
+            dma((8,)),
             dma((3,)),
             dma((3,)),
             pltpu.SemaphoreType.REGULAR,

time: 48.5 us -> 48.6 us (level)
  no operation moved by 1% of the time
where the time goes in v7:
time: 48.6 us; the launch traced here: 48.5 us
  Pallas kernels  47.9 us (99%)
  local copies, waits for them, and re-layouts  0.66 us (1%)
    pallas_call x1, Pallas kernels, per_device(): pl.pallas_call(kernel, out_shape=pltpu.VMEM((128, 256), F32), in_specs=[h...  47.9 us

profile of v7, /device:TPU:1, one launch (start us, length us, event | category | flops | bytes accessed | tf_op | source)
XLA Modules:
  0.0 48.5 jit_solution(13316469255177633191)
XLA Ops:
  0.0 47.9 %schur.1 = f32[128,256]{1,0:T(8,128)S(1)} custom-call(s32[1,2]{1,0:T(1,128)} %owner_hbm.1, s32[1,2,2,8]{3,2,1,0:T(2,128)} %map_hbm.1, s32[1,2]{1,0:T(1,128)} %offset_hbm.1, s32[1,2]{1,0:T(1,128)} %count_hbm.1, bf16[1,1,512,1024]{3,2,1,0:T(8,128)(2,1)} %store_ref.1, bf16[1,2,1024,1024]{3,2,1,0:T(8,128)(2,1)} %inverse_ref.1, ...), custom_call_target="tpu_custom_call" | custom-call | tf_op jit(solution)/shard_map/schur/pallas_call | solution.py:597
  47.9 0.7 %copy.10 = f32[128,256]{1,0:T(8,128)} copy(f32[128,256]{1,0:T(8,128)S(1)} %schur.1) | data formatting | bytes 262144
